TPU v7x, 128 devices: a whole 4x4x4 slice. The times are simulated.
128 devices in a mesh: section: 4 (over z), chan: 32 (over x, y, core).
Axes of the slice: x: 4, y: 4, z: 4, core: 2. Of those that a mesh axis runs over, the one named last changes fastest.
Arguments:
- inputs: bfloat16 [4, 256, 4096], P(None, None, 'chan'), may hold values from -6 to 6
- labels: int32 [4, 256], replicated, may hold values from 0 to 2
- conv_weight: bfloat16 [4, 9, 64, 4096], P('section', None, None, 'chan'), may hold values from -0.25 to 0.25
- point_weight: bfloat16 [4, 4096, 4096], P('section', 'chan'), may hold values from -0.1875 to 0.1875
- head_weight: bfloat16 [4096, 3], P('chan'), may hold values from -0.09375 to 0.09375
Outputs:
- grad_point: float32 [4, 4096, 4096], P('section', 'chan')
- grad_conv: float32 [4, 9, 64, 4096], P('section', None, None, 'chan')
All inputs are finite; a program needn't handle non-finite values.
Results may differ from a plain program's by a relative error of at most 0.035.
Values may be sent and summed in bfloat16 or wider, within the bound.
A program may use at most 128 MiB of HBM per device.

v0:
```python
import jax
import jax.numpy as jnp
from jax import lax
from jax.sharding import PartitionSpec as P

CLASSES = 3
LOSS_SCALE = 2048


def from_behind(value, axis, steps):
    count = lax.axis_size(axis)
    leading, last = (max(0, -steps), min(count, count - steps))
    return lax.ppermute(value, axis, [(source, source + steps) for source in range(leading, last)])


def conv_local(field, kernel, groups):
    half = kernel.shape[0] // 2
    return lax.conv_general_dilated(
        field[None],
        kernel,
        (1,),
        [(half, half)],
        dimension_numbers=("NWC", "WIO", "NWC"),
        feature_group_count=groups,
        preferred_element_type=jnp.float32,
    )[0]


def turn_kernel(kernel):
    taps, width, chans = kernel.shape
    shaped = kernel.reshape(taps, width, chans // width, width)
    shaped = jnp.transpose(shaped, (0, 3, 2, 1))[::-1]
    return shaped.reshape(taps, width, chans)


def kernel_grad(field, grads, width, taps):
    half = taps // 2
    steps, chans = field.shape
    padded = jnp.pad(field, ((half, half), (0, 0)))
    grads3 = grads.reshape(steps, chans // width, width)
    pieces = []
    for k in range(taps):
        shifted = padded[k : k + steps].reshape(steps, chans // width, width)
        pieces.append(
            jnp.einsum("tgi,tgo->igo", shifted, grads3, preferred_element_type=jnp.float32).reshape(
                width, chans
            )
        )
    return jnp.stack(pieces)


def local(inputs, labels, conv_weight, point_weight, head_weight):
    micro, steps, local_chans = inputs.shape
    blocks_here, taps, width, unused_chans = conv_weight.shape
    groups = local_chans // width
    section = lax.axis_index("section")
    n_section = lax.axis_size("section")
    last = n_section - 1
    rounds = micro + n_section - 1
    head32 = head_weight.astype(jnp.float32)
    kernels = [conv_weight[0]]
    turned = [turn_kernel(kernels[0])]
    saved = jnp.zeros((blocks_here, micro, steps, local_chans), jnp.bfloat16)
    top_saved = jnp.zeros((micro, steps, local_chans), jnp.bfloat16)
    received = jnp.zeros((steps, local_chans), jnp.bfloat16)
    for step in range(rounds):
        index = step - section
        valid = (index >= 0) & (index < micro)
        clipped = jnp.clip(index, 0, micro - 1)
        state = jnp.where(
            section == 0, lax.dynamic_index_in_dim(inputs, clipped, 0, keepdims=False), received
        )
        b = 0
        slot = jnp.where(
            valid, lax.dynamic_update_index_in_dim(saved[b], state, clipped, 0), saved[b]
        )
        saved = saved.at[b].set(slot)
        conv_out = conv_local(state, kernels[b], groups)
        act = (conv_out * jax.nn.sigmoid(conv_out)).astype(jnp.bfloat16)
        weight_now = point_weight[b]
        partial_mix = jnp.dot(act, weight_now, preferred_element_type=jnp.float32)
        mixed = lax.psum_scatter(
            partial_mix.astype(jnp.bfloat16), "chan", scatter_dimension=1, tiled=True
        ).astype(jnp.float32)
        state = (state.astype(jnp.float32) + mixed).astype(jnp.bfloat16)
        scores = lax.psum(jnp.dot(state, head_weight, preferred_element_type=jnp.float32), "chan")
        label_row = lax.dynamic_index_in_dim(labels, clipped, 0, keepdims=False)
        onehot = (label_row[:, None] == jnp.arange(CLASSES)[None, :]).astype(jnp.float32)
        top = (jax.nn.sigmoid(scores) - onehot) * (LOSS_SCALE / (micro * steps))
        back_top = jnp.dot(top, head32.T, precision=lax.Precision.HIGHEST).astype(jnp.bfloat16)
        top_saved = jnp.where(
            valid & (section == last),
            lax.dynamic_update_index_in_dim(top_saved, back_top, clipped, 0),
            top_saved,
        )
        if step + 1 < rounds:
            received = from_behind(state, "section", 1)
    grad_point = [jnp.zeros(point_weight.shape[1:], jnp.float32)]
    grad_conv = [jnp.zeros(conv_weight.shape[1:], jnp.float32)]
    received = jnp.zeros((steps, local_chans), jnp.bfloat16)
    for step in range(rounds):
        index = step - (last - section)
        valid = (index >= 0) & (index < micro)
        clipped = jnp.clip(index, 0, micro - 1)
        back = jnp.where(
            section == last,
            lax.dynamic_index_in_dim(top_saved, clipped, 0, keepdims=False),
            received,
        )
        b = 0
        state_b = lax.dynamic_index_in_dim(saved[b], clipped, 0, keepdims=False)
        conv_out = conv_local(state_b, kernels[b], groups)
        sig = jax.nn.sigmoid(conv_out)
        act = jnp.where(valid, (conv_out * sig).astype(jnp.bfloat16), jnp.zeros_like(state_b))
        weight_rows = point_weight[b]

        def fold_grad(carry, piece, start, act=act, weight_rows=weight_rows):
            act_grad, grad_rows_acc = carry
            count = piece.shape[1]
            columns = lax.dynamic_slice_in_dim(weight_rows, start, count, 1)
            act_grad = act_grad + lax.dot_general(
                piece, columns, (((1,), (1,)), ((), ())), preferred_element_type=jnp.float32
            )
            old = lax.dynamic_slice_in_dim(grad_rows_acc, start, count, 1)
            fresh = old + lax.dot_general(
                act, piece, (((0,), (0,)), ((), ())), preferred_element_type=jnp.float32
            )
            return (act_grad, lax.dynamic_update_slice_in_dim(grad_rows_acc, fresh, start, 1))

        start_grad = jnp.zeros((steps, local_chans), jnp.float32)
        act_grad, grad_point[b] = fold_grad(
            (start_grad, grad_point[b]),
            lax.all_gather(back, "chan", axis=1, tiled=True),
            jnp.int32(0),
        )
        conv_grad = jnp.where(
            valid,
            (act_grad * sig * (1.0 + conv_out * (1.0 - sig))).astype(jnp.bfloat16),
            jnp.zeros_like(state_b),
        )
        grad_conv[b] = grad_conv[b] + kernel_grad(state_b, conv_grad, width, taps)
        input_grad = conv_local(conv_grad, turned[b], groups)
        back = (back.astype(jnp.float32) + input_grad).astype(jnp.bfloat16)
        if step + 1 < rounds:
            received = from_behind(back, "section", -1)
    return (jnp.stack(grad_point), jnp.stack(grad_conv))


def solution(mesh):
    placed = (
        P(None, None, "chan"),
        P(),
        P("section", None, None, "chan"),
        P("section", "chan", None),
        P("chan", None),
    )
    return jax.shard_map(
        local,
        mesh=mesh,
        in_specs=placed,
        out_specs=(P("section", "chan", None), P("section", None, None, "chan")),
        check_vma=False,
    )
```

profile of v0, /device:TPU:1, one launch (start us, length us, event | category | flops | bytes accessed | tf_op | source)
XLA Modules:
  0.0 1214.2 jit_solution(8191468728960456842)
XLA Ops:
  14.8 80.3 %reduce-scatter.22.cloned.1.call-done = bf16[128,256]{1,0:T(8,128)(2,1)} async-done(((bf16[4096,256]{1,0:T(8,128)(2,1)}), bf16[128,256]{1,0:T(8,128)(2,1)}) %reduce-scatter.22.cloned.1.call-update) | async-done | bytes 65552
  96.0 3.2 collective-permute-start
  108.2 79.0 %reduce-scatter.24.cloned.1.call-done = bf16[128,256]{1,0:T(8,128)(2,1)} async-done(((bf16[4096,256]{1,0:T(8,128)(2,1)}), bf16[128,256]{1,0:T(8,128)(2,1)}) %reduce-scatter.24.cloned.1.call-update) | async-done | bytes 65552
  188.2 3.2 collective-permute-start.1
  196.9 2.5 copy.956
  200.3 79.0 %reduce-scatter.26.cloned.1.call-done = bf16[128,256]{1,0:T(8,128)(2,1)} async-done(((bf16[4096,256]{1,0:T(8,128)(2,1)}), bf16[128,256]{1,0:T(8,128)(2,1)}) %reduce-scatter.26.cloned.1.call-update) | async-done | bytes 65552
  280.3 3.7 collective-permute-start.2
  289.0 2.5 copy.958
  292.5 79.0 %reduce-scatter.28.cloned.1.call-done = bf16[128,256]{1,0:T(8,128)(2,1)} async-done(((bf16[4096,256]{1,0:T(8,128)(2,1)}), bf16[128,256]{1,0:T(8,128)(2,1)}) %reduce-scatter.28.cloned.1.call-update) | async-done | bytes 65552
  372.4 3.2 collective-permute-start.3
  384.6 78.9 %reduce-scatter.30.cloned.1.call-done = bf16[128,256]{1,0:T(8,128)(2,1)} async-done(((bf16[4096,256]{1,0:T(8,128)(2,1)}), bf16[128,256]{1,0:T(8,128)(2,1)}) %reduce-scatter.30.cloned.1.call-update) | async-done | bytes 65552
  464.6 3.2 collective-permute-start.4
  476.7 78.9 %reduce-scatter.32.cloned.1.call-done = bf16[128,256]{1,0:T(8,128)(2,1)} async-done(((bf16[4096,256]{1,0:T(8,128)(2,1)}), bf16[128,256]{1,0:T(8,128)(2,1)}) %reduce-scatter.32.cloned.1.call-update) | async-done | bytes 65552
  556.6 3.3 collective-permute-start.5
  569.4 78.4 %reduce-scatter.34.cloned.1.call-done = bf16[128,256]{1,0:T(8,128)(2,1)} async-done(((bf16[4096,256]{1,0:T(8,128)(2,1)}), bf16[128,256]{1,0:T(8,128)(2,1)}) %reduce-scatter.34.cloned.1.call-update) | async-done | bytes 65552
  648.9 120.9 %all-reduce.7 = (f32[256,3]{0,1:T(4,128)S(1)}, f32[256,3]{0,1:T(4,128)S(1)}, f32[256,3]{0,1:T(4,128)S(1)}, f32[256,3]{0,1:T(4,128)S(1)}, f32[256,3]{0,1:T(4,128)...) all-reduce(f32[256,3]{0,1:T(4,128)S(1)} %fusion.205, ...), channel_id=1, replica_groups=mesh['section'=4,'chan'=32] {'chan'}, use_global_device_ids=true, to_apply=%region_6.7 | all-reduce | flops 5376 | bytes 43008 | tf_op jit(solution)/shard_map/psum | solution.py:86
  775.2 44.3 %all-gather.21.cloned.1.call-done = bf16[1,256,4096]{2,1,0:T(8,128)(2,1)} async-done(((bf16[1,256,128]{2,1,0:T(8,128)(2,1)}), bf16[1,256,4096]{2,1,0:T(8,128)(2,1)}) %all-gather.21.cloned.1.call-update) | async-done | bytes 2097168 | tf_op jit(solution)/shard_map/all_gather | solution.py:133
  825.6 3.7 collective-permute-done.6
  836.5 38.9 %all-gather.9.cloned.1.call-done = bf16[256,4096]{1,0:T(8,128)(2,1)} async-done(((bf16[256,128]{1,0:T(8,128)(2,1)}), bf16[256,4096]{1,0:T(8,128)(2,1)}) %all-gather.9.cloned.1.call-update) | async-done | bytes 2097168 | tf_op jit(solution)/shard_map/all_gather | solution.py:133
  947.0 3.1 collective-permute-done.8
  983.7 3.5 convolution_add_fusion.1
  987.4 9.9 all-gather.13.cloned.1.call-done
  1003.7 3.5 collective-permute-done.9
  1011.1 42.2 %all-gather.15.cloned.1.call-done = bf16[256,4096]{1,0:T(8,128)(2,1)} async-done(((bf16[256,128]{1,0:T(8,128)(2,1)}), bf16[256,4096]{1,0:T(8,128)(2,1)}) %all-gather.15.cloned.1.call-update) | async-done | bytes 2097168 | tf_op jit(solution)/shard_map/all_gather | solution.py:133
  1059.6 3.6 collective-permute-done.10
  1098.9 10.2 all-gather.17.cloned.1.call-done
  1112.5 3.7 fusion.204
  1130.3 3.6 fusion.87
  1161.3 3.5 fusion.85
  1164.8 6.8 all-gather.19.cloned.1.call-done
  1171.6 2.9 fusion.42
  1203.4 4.0 fusion.4
  (660 shorter events, 310.6 us)
Async XLA Ops:
  7.2 87.9 %reduce-scatter.22.cloned.1.call-start = ((), (), s32[]{:S(2)}) async-start(), calls=%async_computation.14 | async-start | bytes 2162688
  14.5 172.6 %reduce-scatter.24.cloned.1.call-start = ((), (), s32[]{:S(2)}) async-start(), calls=%async_computation.15 | async-start | bytes 2162688
  96.0 4.5 collective-permute-start
  107.2 172.1 %reduce-scatter.26.cloned.1.call-start = ((), (), s32[]{:S(2)}) async-start(), calls=%async_computation.16 | async-start | bytes 2162688
  188.2 4.5 collective-permute-start.1
  199.4 172.1 %reduce-scatter.28.cloned.1.call-start = ((), (), s32[]{:S(2)}) async-start(), calls=%async_computation.17 | async-start | bytes 2162688
  280.3 4.5 collective-permute-start.2
  291.5 172.0 %reduce-scatter.30.cloned.1.call-start = ((), (), s32[]{:S(2)}) async-start(), calls=%async_computation.18 | async-start | bytes 2162688
  372.4 4.5 collective-permute-start.3
  383.7 172.0 %reduce-scatter.32.cloned.1.call-start = ((), (), s32[]{:S(2)}) async-start(), calls=%async_computation.19 | async-start | bytes 2162688
  464.6 4.5 collective-permute-start.4
  475.7 172.1 %reduce-scatter.34.cloned.1.call-start = ((), (), s32[]{:S(2)}) async-start(), calls=%async_computation.20 | async-start | bytes 2162688
  556.6 4.5 collective-permute-start.5
  567.8 205.2 %copy-start.70 = (bf16[1,1,256,128]{3,2,1,0:T(8,128)(2,1)S(1)}, bf16[1,1,256,128]{3,2,1,0:T(8,128)(2,1)}, u32[]{:S(2)}) copy-start(bf16[1,1,256,128]{3,2,1,0:T(8,128)(2,1)} %get-tuple-element.93) | copy-start | bytes 196612
  567.9 205.6 %copy-start.38 = (bf16[9,64,2,64]{3,1,2,0:T(8,128)(2,1)S(1)}, bf16[9,64,2,64]{3,1,2,0:T(8,128)(2,1)}, u32[]{:S(2)}) copy-start(bf16[9,64,2,64]{3,1,2,0:T(8,128)(2,1)} %copy-done.31) | copy-start | bytes 442372
  567.9 251.6 %all-gather.21.cloned.1.call-start = ((), (), s32[]{:S(2)}) async-start(), calls=%async_computation.13 | async-start | bytes 2162688 | tf_op jit(solution)/shard_map/all_gather | solution.py:133
  772.2 177.9 %copy-start.4 = (bf16[4,256,128]{2,1,0:T(8,128)(2,1)}, bf16[4,256,128]{2,1,0:T(8,128)(2,1)S(1)}, u32[]{:S(2)}) copy-start(bf16[4,256,128]{2,1,0:T(8,128)(2,1)S(1)} %fusion.49) | copy-start | bytes 786436
  772.9 102.4 %all-gather.9.cloned.1.call-start = ((), (), s32[]{:S(2)}) async-start(), calls=%async_computation.7 | async-start | bytes 2162688 | tf_op jit(solution)/shard_map/all_gather | solution.py:133
  773.2 115.5 %copy-start.12 = (bf16[1,1,256,128]{2,3,1,0:T(8,128)(2,1)}, bf16[1,1,256,128]{2,3,1,0:T(8,128)(2,1)S(1)}, u32[]{:S(2)}) copy-start(bf16[1,1,256,128]{2,3,1,0:T(8,128)(2,1)S(1)} %get-tuple-element.110) | copy-start | bytes 196612
  773.3 115.6 %copy-start.14 = (bf16[1,1,256,128]{2,3,1,0:T(8,128)(2,1)}, bf16[1,1,256,128]{2,3,1,0:T(8,128)(2,1)S(1)}, u32[]{:S(2)}) copy-start(bf16[1,1,256,128]{2,3,1,0:T(8,128)(2,1)S(1)} %get-tuple-element.111) | copy-start | bytes 196612
  773.3 121.8 %copy-start.6 = (bf16[1,1,256,128]{2,3,1,0:T(8,128)(2,1)}, bf16[1,1,256,128]{2,3,1,0:T(8,128)(2,1)S(1)}, u32[]{:S(2)}) copy-start(bf16[1,1,256,128]{2,3,1,0:T(8,128)(2,1)S(1)} %get-tuple-element.107) | copy-start | bytes 196612
  824.3 5.0 collective-permute-start.6
  830.0 110.3 %all-gather.11.cloned.1.call-start = ((), (), s32[]{:S(2)}) async-start(), calls=%async_computation.8 | async-start | bytes 2162688 | tf_op jit(solution)/shard_map/all_gather | solution.py:133
  880.1 5.0 collective-permute-start.7
  885.8 111.5 %all-gather.13.cloned.1.call-start = ((), (), s32[]{:S(2)}) async-start(), calls=%async_computation.9 | async-start | bytes 2162688 | tf_op jit(solution)/shard_map/all_gather | solution.py:133
  945.1 5.0 collective-permute-start.8
  950.7 102.6 %all-gather.15.cloned.1.call-start = ((), (), s32[]{:S(2)}) async-start(), calls=%async_computation.10 | async-start | bytes 2162688 | tf_op jit(solution)/shard_map/all_gather | solution.py:133
  1002.3 5.0 collective-permute-start.9
  1007.9 101.3 %all-gather.17.cloned.1.call-start = ((), (), s32[]{:S(2)}) async-start(), calls=%async_computation.11 | async-start | bytes 2162688 | tf_op jit(solution)/shard_map/all_gather | solution.py:133
  1058.2 5.0 collective-permute-start.10
  1063.8 107.8 %all-gather.19.cloned.1.call-start = ((), (), s32[]{:S(2)}) async-start(), calls=%async_computation.12 | async-start | bytes 2162688 | tf_op jit(solution)/shard_map/all_gather | solution.py:133
  1120.5 5.0 collective-permute-start.11
  (76 other events, 1448.0 us)
Sparse Core Ops, SparseCore 0:
  14.7 80.3 reduce-scatter.21
  107.3 79.7 reduce-scatter.23
  199.5 79.7 reduce-scatter.25
  291.6 79.7 reduce-scatter.27
  383.8 79.7 reduce-scatter.29
  475.9 79.7 reduce-scatter.31
  568.0 79.7 reduce-scatter.33
  773.1 46.3 all-gather.20
  830.1 45.2 all-gather.8
  885.9 45.2 all-gather.10
  950.9 46.3 all-gather.12
  1008.0 45.2 all-gather.14
  1063.9 45.2 all-gather.16
  1126.3 45.2 all-gather.18
where the time goes:
time: 1230 us; the launch traced here: 1210 us
  waiting for transfers between devices  730 us (59%)
  local copies, waits for them, and re-layouts  175 us (14%)
  matrix products  124 us (10%)
  blocking collectives  121 us (10%)
  starting transfers between devices  29 us (2%)
  other arithmetic  18.1 us (1%)
  between operations  17.1 us (1%)
    unnamed x21, waiting for transfers between devices  554 us
    all_gather x7, waiting for transfers between devices, local(): lax.all_gather(back, 'chan', axis=1, tiled=True)  152 us
    psum x1, blocking collectives, local(): lax.psum(jnp.dot(state, head_weight, preferred_element_type=jnp.float32),...  121 us
    unnamed x234, local copies, waits for them, and re-layouts  71.9 us
    another operation x70, local copies, waits for them, and re-layouts, kernel_grad(): return jnp.stack(pieces)  44.8 us
    dot_general x63, matrix products, kernel_grad(): jnp.einsum('tgi,tgo->igo', shifted, grads3, preferred_element_type=jnp.fl...  41.1 us
    conv_general_dilated x20, matrix products, conv_local(): lax.conv_general_dilated(field[None], kernel, (1,), [(half, half)], dimen...  37 us
    slice x63, local copies, waits for them, and re-layouts, kernel_grad(): shifted = padded[k:k + steps].reshape(steps, chans // width, width)  36 us
  transfers between devices with their start and end apart: 26, of which 25 were waited for; matrix products, arithmetic and copies ran while one was open for 15% of the time, Pallas kernels for 0%

commit v1 on v0

--- a/solution.py
+++ b/solution.py
@@ -5,6 +5,12 @@
 
 CLASSES = 3
 LOSS_SCALE = 2048
+
+
+def summed_here(x, axis):
+    blocks = lax.all_gather(x, axis, axis=0, tiled=False)
+    total = blocks.sum(axis=0)
+    return total
 
 
 def from_behind(value, axis, steps):
@@ -83,7 +89,9 @@
             partial_mix.astype(jnp.bfloat16), "chan", scatter_dimension=1, tiled=True
         ).astype(jnp.float32)
         state = (state.astype(jnp.float32) + mixed).astype(jnp.bfloat16)
-        scores = lax.psum(jnp.dot(state, head_weight, preferred_element_type=jnp.float32), "chan")
+        scores = summed_here(
+            jnp.dot(state, head_weight, preferred_element_type=jnp.float32), "chan"
+        )
         label_row = lax.dynamic_index_in_dim(labels, clipped, 0, keepdims=False)
         onehot = (label_row[:, None] == jnp.arange(CLASSES)[None, :]).astype(jnp.float32)
         top = (jax.nn.sigmoid(scores) - onehot) * (LOSS_SCALE / (micro * steps))

time: 1230 us -> 1170 us (0.951)
  waiting for transfers between devices: 730 us -> 622 us
  blocking collectives: 121 us -> 169 us
    all_gather x0 -> x7, blocking collectives: none -> 169 us  [summed_here(): blocks = lax.all_gather(x, axis, axis=0, tiled=False)]
    psum x1 -> x0, blocking collectives: 121 us -> none  [local(): lax.psum(jnp.dot(state, head_weight, preferred_element_type=jnp.float32),...]
    unnamed x21, waiting for transfers between devices: 554 us -> 449 us
    unnamed x234 -> x242, local copies, waits for them, and re-layouts: 71.9 us -> 71.1 us
  transfers between devices with their start and end apart: 26 -> 26, of which waited for: 25 -> 24; matrix products, arithmetic and copies ran while one was open for 15% -> 16% of each run, Pallas kernels for 0% -> 0%
where the time goes in v1:
time: 1170 us; the launch traced here: 1160 us
  waiting for transfers between devices  622 us (53%)
  local copies, waits for them, and re-layouts  175 us (15%)
  blocking collectives  169 us (14%)
  matrix products  124 us (11%)
  starting transfers between devices  29.1 us (2%)
  other arithmetic  17.8 us (2%)
  between operations  17.4 us (1%)
    unnamed x21, waiting for transfers between devices  449 us
    all_gather x7, blocking collectives, summed_here(): blocks = lax.all_gather(x, axis, axis=0, tiled=False)  169 us
    all_gather x7, waiting for transfers between devices, local(): lax.all_gather(back, 'chan', axis=1, tiled=True)  150 us
    unnamed x242, local copies, waits for them, and re-layouts  71.1 us
    another operation x70, local copies, waits for them, and re-layouts, kernel_grad(): return jnp.stack(pieces)  45.1 us
    dot_general x63, matrix products, kernel_grad(): jnp.einsum('tgi,tgo->igo', shifted, grads3, preferred_element_type=jnp.fl...  41.1 us
    conv_general_dilated x20, matrix products, conv_local(): lax.conv_general_dilated(field[None], kernel, (1,), [(half, half)], dimen...  37.1 us
    slice x63, local copies, waits for them, and re-layouts, kernel_grad(): shifted = padded[k:k + steps].reshape(steps, chans // width, width)  36.4 us
  transfers between devices with their start and end apart: 26, of which 24 were waited for; matrix products, arithmetic and copies ran while one was open for 16% of the time, Pallas kernels for 0%

profile of v1, /device:TPU:1, one launch (start us, length us, event | category | flops | bytes accessed | tf_op | source)
XLA Modules:
  0.0 1155.1 jit_solution(9836524677596589428)
XLA Ops:
  14.8 80.3 %reduce-scatter.22.cloned.1.call-done = bf16[128,256]{1,0:T(8,128)(2,1)} async-done(((bf16[4096,256]{1,0:T(8,128)(2,1)}), bf16[128,256]{1,0:T(8,128)(2,1)}) %reduce-scatter.22.cloned.1.call-update) | async-done | bytes 65552
  96.0 3.2 collective-permute-start
  106.8 79.8 %reduce-scatter.24.cloned.1.call-done = bf16[128,256]{1,0:T(8,128)(2,1)} async-done(((bf16[4096,256]{1,0:T(8,128)(2,1)}), bf16[128,256]{1,0:T(8,128)(2,1)}) %reduce-scatter.24.cloned.1.call-update) | async-done | bytes 65552
  199.7 79.0 %reduce-scatter.26.cloned.1.call-done = bf16[128,256]{1,0:T(8,128)(2,1)} async-done(((bf16[4096,256]{1,0:T(8,128)(2,1)}), bf16[128,256]{1,0:T(8,128)(2,1)}) %reduce-scatter.26.cloned.1.call-update) | async-done | bytes 65552
  279.7 3.7 collective-permute-start.2
  291.9 78.9 %reduce-scatter.28.cloned.1.call-done = bf16[128,256]{1,0:T(8,128)(2,1)} async-done(((bf16[4096,256]{1,0:T(8,128)(2,1)}), bf16[128,256]{1,0:T(8,128)(2,1)}) %reduce-scatter.28.cloned.1.call-update) | async-done | bytes 65552
  371.8 3.2 collective-permute-start.3
  384.0 79.0 %reduce-scatter.30.cloned.1.call-done = bf16[128,256]{1,0:T(8,128)(2,1)} async-done(((bf16[4096,256]{1,0:T(8,128)(2,1)}), bf16[128,256]{1,0:T(8,128)(2,1)}) %reduce-scatter.30.cloned.1.call-update) | async-done | bytes 65552
  464.0 3.2 collective-permute-start.4
  476.6 26.9 %all-gather = f32[8192,3]{0,1:T(4,128)S(1)} all-gather(f32[256,3]{0,1:T(4,128)S(1)} %fusion.205), channel_id=2, replica_groups=mesh['section'=4,'chan'=32] {'chan'}, dimensions={0}, use_global_device_ids=true | all-gather | bytes 101376 | tf_op jit(solution)/shard_map/all_gather | solution.py:11
  503.7 51.5 %reduce-scatter.32.cloned.1.call-done = bf16[128,256]{1,0:T(8,128)(2,1)} async-done(((bf16[4096,256]{1,0:T(8,128)(2,1)}), bf16[128,256]{1,0:T(8,128)(2,1)}) %reduce-scatter.32.cloned.1.call-update) | async-done | bytes 65552
  556.1 3.4 collective-permute-start.5
  568.4 26.9 %all-gather.1 = f32[8192,3]{0,1:T(4,128)S(1)} all-gather(f32[256,3]{0,1:T(4,128)S(1)} %fusion.206), channel_id=3, replica_groups=mesh['section'=4,'chan'=32] {'chan'}, dimensions={0}, use_global_device_ids=true | all-gather | bytes 101376 | tf_op jit(solution)/shard_map/all_gather | solution.py:11
  595.8 22.4 %all-gather.2 = f32[8192,3]{0,1:T(4,128)S(1)} all-gather(f32[256,3]{0,1:T(4,128)S(1)} %fusion.207), channel_id=4, replica_groups=mesh['section'=4,'chan'=32] {'chan'}, dimensions={0}, use_global_device_ids=true | all-gather | bytes 101376 | tf_op jit(solution)/shard_map/all_gather | solution.py:11
  618.7 23.9 %all-gather.3 = f32[8192,3]{0,1:T(4,128)S(1)} all-gather(f32[256,3]{0,1:T(4,128)S(1)} %fusion.208), channel_id=5, replica_groups=mesh['section'=4,'chan'=32] {'chan'}, dimensions={0}, use_global_device_ids=true | all-gather | bytes 101376 | tf_op jit(solution)/shard_map/all_gather | solution.py:11
  643.2 22.4 %all-gather.4 = f32[8192,3]{0,1:T(4,128)S(1)} all-gather(f32[256,3]{0,1:T(4,128)S(1)} %fusion.209), channel_id=6, replica_groups=mesh['section'=4,'chan'=32] {'chan'}, dimensions={0}, use_global_device_ids=true | all-gather | bytes 101376 | tf_op jit(solution)/shard_map/all_gather | solution.py:11
  666.0 23.9 %all-gather.5 = f32[8192,3]{0,1:T(4,128)S(1)} all-gather(f32[256,3]{0,1:T(4,128)S(1)} %fusion.210), channel_id=7, replica_groups=mesh['section'=4,'chan'=32] {'chan'}, dimensions={0}, use_global_device_ids=true | all-gather | bytes 101376 | tf_op jit(solution)/shard_map/all_gather | solution.py:11
  691.5 22.4 %all-gather.6 = f32[8192,3]{0,1:T(4,128)S(1)} all-gather(f32[256,3]{0,1:T(4,128)S(1)} %fusion.76), channel_id=8, replica_groups=mesh['section'=4,'chan'=32] {'chan'}, dimensions={0}, use_global_device_ids=true | all-gather | bytes 101376 | tf_op jit(solution)/shard_map/all_gather | solution.py:11
  717.6 41.9 %all-gather.28.cloned.1.call-done = bf16[1,256,4096]{2,1,0:T(8,128)(2,1)} async-done(((bf16[1,256,128]{2,1,0:T(8,128)(2,1)}), bf16[1,256,4096]{2,1,0:T(8,128)(2,1)}) %all-gather.28.cloned.1.call-update) | async-done | bytes 2097168 | tf_op jit(solution)/shard_map/all_gather | solution.py:141
  765.7 3.7 collective-permute-done.6
  776.4 39.1 %all-gather.16.cloned.1.call-done = bf16[256,4096]{1,0:T(8,128)(2,1)} async-done(((bf16[256,128]{1,0:T(8,128)(2,1)}), bf16[256,4096]{1,0:T(8,128)(2,1)}) %all-gather.16.cloned.1.call-update) | async-done | bytes 2097168 | tf_op jit(solution)/shard_map/all_gather | solution.py:141
  924.4 3.6 convolution_add_fusion.1
  928.1 9.6 all-gather.20.cloned.1.call-done
  944.2 3.5 collective-permute-done.9
  951.5 42.2 %all-gather.22.cloned.1.call-done = bf16[256,4096]{1,0:T(8,128)(2,1)} async-done(((bf16[256,128]{1,0:T(8,128)(2,1)}), bf16[256,4096]{1,0:T(8,128)(2,1)}) %all-gather.22.cloned.1.call-update) | async-done | bytes 2097168 | tf_op jit(solution)/shard_map/all_gather | solution.py:141
  1000.0 3.6 collective-permute-done.10
  1039.6 10.0 all-gather.24.cloned.1.call-done
  1052.9 3.7 fusion.204
  1070.8 3.6 fusion.87
  1101.9 3.5 fusion.85
  1105.4 6.7 all-gather.26.cloned.1.call-done
  1144.0 4.0 fusion.4
  (681 shorter events, 325.0 us)
Async XLA Ops:
  7.2 87.9 %reduce-scatter.22.cloned.1.call-start = ((), (), s32[]{:S(2)}) async-start(), calls=%async_computation.14 | async-start | bytes 2162688
  14.5 172.0 %reduce-scatter.24.cloned.1.call-start = ((), (), s32[]{:S(2)}) async-start(), calls=%async_computation.15 | async-start | bytes 2162688
  96.0 4.5 collective-permute-start
  106.6 172.1 %reduce-scatter.26.cloned.1.call-start = ((), (), s32[]{:S(2)}) async-start(), calls=%async_computation.16 | async-start | bytes 2162688
  187.6 4.5 collective-permute-start.1
  198.8 172.1 %reduce-scatter.28.cloned.1.call-start = ((), (), s32[]{:S(2)}) async-start(), calls=%async_computation.17 | async-start | bytes 2162688
  279.7 4.5 collective-permute-start.2
  290.9 172.0 %reduce-scatter.30.cloned.1.call-start = ((), (), s32[]{:S(2)}) async-start(), calls=%async_computation.18 | async-start | bytes 2162688
  371.8 4.5 collective-permute-start.3
  383.0 172.1 %reduce-scatter.32.cloned.1.call-start = ((), (), s32[]{:S(2)}) async-start(), calls=%async_computation.19 | async-start | bytes 2162688
  464.0 4.5 collective-permute-start.4
  475.2 215.2 %reduce-scatter.34.cloned.1.call-start = ((), (), s32[]{:S(2)}) async-start(), calls=%async_computation.20 | async-start | bytes 2162688
  556.1 4.5 collective-permute-start.5
  567.4 148.0 %copy-start.72 = (bf16[1,1,256,128]{3,2,1,0:T(8,128)(2,1)S(1)}, bf16[1,1,256,128]{3,2,1,0:T(8,128)(2,1)}, u32[]{:S(2)}) copy-start(bf16[1,1,256,128]{3,2,1,0:T(8,128)(2,1)} %get-tuple-element.86) | copy-start | bytes 196612
  567.5 192.1 %all-gather.28.cloned.1.call-start = ((), (), s32[]{:S(2)}) async-start(), calls=%async_computation.13 | async-start | bytes 2162688 | tf_op jit(solution)/shard_map/all_gather | solution.py:141
  714.2 176.3 %copy-start.4 = (bf16[4,256,128]{2,1,0:T(8,128)(2,1)}, bf16[4,256,128]{2,1,0:T(8,128)(2,1)S(1)}, u32[]{:S(2)}) copy-start(bf16[4,256,128]{2,1,0:T(8,128)(2,1)S(1)} %fusion.49) | copy-start | bytes 786436
  715.0 100.5 %all-gather.16.cloned.1.call-start = ((), (), s32[]{:S(2)}) async-start(), calls=%async_computation.7 | async-start | bytes 2162688 | tf_op jit(solution)/shard_map/all_gather | solution.py:141
  715.6 112.9 %copy-start.10 = (bf16[1,1,256,128]{2,3,1,0:T(8,128)(2,1)}, bf16[1,1,256,128]{2,3,1,0:T(8,128)(2,1)S(1)}, u32[]{:S(2)}) copy-start(bf16[1,1,256,128]{2,3,1,0:T(8,128)(2,1)S(1)} %get-tuple-element.102) | copy-start | bytes 196612
  715.7 113.0 %copy-start.12 = (bf16[1,1,256,128]{2,3,1,0:T(8,128)(2,1)}, bf16[1,1,256,128]{2,3,1,0:T(8,128)(2,1)S(1)}, u32[]{:S(2)}) copy-start(bf16[1,1,256,128]{2,3,1,0:T(8,128)(2,1)S(1)} %get-tuple-element.103) | copy-start | bytes 196612
  715.7 113.1 %copy-start.14 = (bf16[1,1,256,128]{2,3,1,0:T(8,128)(2,1)}, bf16[1,1,256,128]{2,3,1,0:T(8,128)(2,1)S(1)}, u32[]{:S(2)}) copy-start(bf16[1,1,256,128]{2,3,1,0:T(8,128)(2,1)S(1)} %get-tuple-element.104) | copy-start | bytes 196612
  715.7 119.3 %copy-start.6 = (bf16[1,1,256,128]{2,3,1,0:T(8,128)(2,1)}, bf16[1,1,256,128]{2,3,1,0:T(8,128)(2,1)S(1)}, u32[]{:S(2)}) copy-start(bf16[1,1,256,128]{2,3,1,0:T(8,128)(2,1)S(1)} %get-tuple-element.100) | copy-start | bytes 196612
  764.4 5.0 collective-permute-start.6
  770.0 110.6 %all-gather.18.cloned.1.call-start = ((), (), s32[]{:S(2)}) async-start(), calls=%async_computation.8 | async-start | bytes 2162688 | tf_op jit(solution)/shard_map/all_gather | solution.py:141
  820.2 5.0 collective-permute-start.7
  825.9 111.8 %all-gather.20.cloned.1.call-start = ((), (), s32[]{:S(2)}) async-start(), calls=%async_computation.9 | async-start | bytes 2162688 | tf_op jit(solution)/shard_map/all_gather | solution.py:141
  885.5 5.0 collective-permute-start.8
  891.2 102.6 %all-gather.22.cloned.1.call-start = ((), (), s32[]{:S(2)}) async-start(), calls=%async_computation.10 | async-start | bytes 2162688 | tf_op jit(solution)/shard_map/all_gather | solution.py:141
  942.7 5.0 collective-permute-start.9
  948.4 101.3 %all-gather.24.cloned.1.call-start = ((), (), s32[]{:S(2)}) async-start(), calls=%async_computation.11 | async-start | bytes 2162688 | tf_op jit(solution)/shard_map/all_gather | solution.py:141
  998.6 5.0 collective-permute-start.10
  1004.3 107.8 %all-gather.26.cloned.1.call-start = ((), (), s32[]{:S(2)}) async-start(), calls=%async_computation.12 | async-start | bytes 2162688 | tf_op jit(solution)/shard_map/all_gather | solution.py:141
  1061.0 5.0 collective-permute-start.11
  (80 other events, 1955.3 us)
Sparse Core Ops, SparseCore 0:
  14.7 80.3 reduce-scatter.21
  106.7 79.7 reduce-scatter.23
  198.9 79.7 reduce-scatter.25
  291.0 79.7 reduce-scatter.27
  383.2 79.7 reduce-scatter.29
  475.3 79.7 reduce-scatter.31
  567.6 79.8 reduce-scatter.33
  715.1 44.4 all-gather.27
  770.2 45.2 all-gather.15
  826.1 45.2 all-gather.17
  891.3 46.3 all-gather.19
  948.5 45.2 all-gather.21
  1004.4 45.2 all-gather.23
  1066.8 45.2 all-gather.25
